TPU v7x, 32 devices: a whole 2x2x4 slice. The times are simulated.
32 devices in a mesh: feat: 4 (over x, core), rows: 8 (over z, y).
Axes of the slice: x: 2, y: 2, z: 4, core: 2. Of those that a mesh axis runs over, the one named last changes fastest.
Arguments:
- kernel: float32 [8192, 8192], P('rows', 'feat'), may hold values from -0.06629126 to 5, as said below
- train_feats: float32 [4096, 8192], P('rows', 'feat'), may hold values from -6 to 6
- test_feats: float32 [2048, 8192], P('rows', 'feat'), may hold values from -6 to 6
Outputs:
- factor_state: float32 [8192, 8192], P('rows', 'feat')
- train_state: float32 [4096, 8192], P('rows', 'feat')
- test_state: float32 [2048, 8192], P('rows', 'feat')
- scores: float32 [4096, 2048], P('rows', 'feat')
Inputs may be any that keep to these rules, and one draw needn't show every extreme that they name: kernel is symmetric and positive definite; its diagonal dominates each row's other entries.
All inputs are finite; a program needn't handle non-finite values.
Results may differ from a plain program's by a relative error of at most 0.0001.
Values sent between devices are 32-bit elements; how exact they have to be, the bound alone decides.
A program may use at most 128 MiB of HBM per device.

v0:
```python
import jax
import jax.numpy as jnp
from jax import lax
from jax.sharding import PartitionSpec as P

PANEL = 256
NPAN = 2


def from_root(block, axis, holder):
    block = jnp.where(lax.axis_index(axis) == holder, block, jnp.zeros_like(block))
    return lax.psum(block, axis)


def product(left, right):
    return jnp.dot(left, right, precision=lax.Precision.HIGHEST, preferred_element_type=jnp.float32)


def update_state(state, coords, right_rows):
    return state - product(coords, right_rows.T)


def per_device(kernel, train_feats, test_feats):
    blk_rows, blk_cols = kernel.shape
    row_index = lax.axis_index("rows")
    feat_index = lax.axis_index("feat")
    row_ids = row_index * blk_rows + jnp.arange(blk_rows, dtype=jnp.int32)
    col_ids = feat_index * blk_cols + jnp.arange(blk_cols, dtype=jnp.int32)
    on_panel = feat_index == 0
    identity = jnp.eye(PANEL, dtype=jnp.float32)
    matrix, train_work, test_work = (kernel, train_feats, test_feats)
    train_parts = []
    test_parts = []
    pending = None
    for panel in range(NPAN):
        first_col = panel * PANEL
        last_col = first_col + PANEL
        root_row = first_col // blk_rows
        offset = first_col % blk_rows
        pending = (
            matrix[:, first_col:last_col],
            matrix[offset : offset + PANEL, :],
            train_work[:, first_col:last_col],
            test_work[:, first_col:last_col],
        )
        col_block, row_block, train_block, test_block = pending
        diagonal = from_root(col_block[offset : offset + PANEL], ("feat", "rows"), root_row)
        factor = jnp.linalg.cholesky(diagonal)
        transposed = jax.scipy.linalg.solve_triangular(factor, identity, lower=True).T
        left_rows = jnp.where((row_ids >= first_col)[:, None], product(col_block, transposed), 0.0)
        train_coords = product(train_block, transposed)
        test_coords = product(test_block, transposed)
        left_rows, train_coords, test_coords = (
            from_root(left_rows, "feat", 0),
            from_root(train_coords, "feat", 0),
            from_root(test_coords, "feat", 0),
        )
        right_rows = jnp.where(
            (col_ids >= first_col)[:, None], product(row_block.T, transposed), 0.0
        )
        right_rows = from_root(right_rows, "rows", root_row)
        train_parts.append(train_coords)
        test_parts.append(test_coords)
        pending = None
        matrix = update_state(matrix, left_rows, right_rows)
        matrix = matrix.at[:, first_col:last_col].set(
            jnp.where(on_panel, left_rows, matrix[:, first_col:last_col])
        )
        train_work = update_state(train_work, train_coords, right_rows)
        train_work = train_work.at[:, first_col:last_col].set(
            jnp.where(on_panel, train_coords, train_work[:, first_col:last_col])
        )
        test_work = update_state(test_work, test_coords, right_rows)
        test_work = test_work.at[:, first_col:last_col].set(
            jnp.where(on_panel, test_coords, test_work[:, first_col:last_col])
        )
    coord_span = NPAN * PANEL
    upper = (row_ids[:, None] < coord_span) & (col_ids[None, :] >= coord_span)
    matrix = jnp.where(upper, 0.0, matrix)
    train_all = jnp.concatenate(train_parts, axis=1)
    test_all = jnp.concatenate(test_parts, axis=1)
    groups = lax.axis_size("rows") // lax.axis_size("feat")
    every_test = lax.all_gather(test_all, "rows", axis=0, tiled=True)
    wanted = lax.dynamic_slice_in_dim(
        every_test, feat_index * (groups * test_all.shape[0]), groups * test_all.shape[0], 0
    )
    scores = product(train_all, wanted.T)
    return (matrix, train_work, test_work, scores)


def solution(mesh):
    return jax.shard_map(
        per_device,
        mesh=mesh,
        in_specs=(P("rows", "feat"), P("rows", "feat"), P("rows", "feat")),
        out_specs=(P("rows", "feat"), P("rows", "feat"), P("rows", "feat"), P("rows", "feat")),
        check_vma=False,
    )
```

profile of v0, /device:TPU:31, one launch (start us, length us, event | category | flops | bytes accessed | tf_op | source)
XLA Modules:
  0.0 818.0 jit_solution(4615605893372237384)
XLA Ops:
  7.2 9.3 %copy.9 = f32[1024,2048]{0,1:T(8,128)} copy(f32[1024,2048]{1,0:T(8,128)} %param.18) | data formatting | bytes 16777216 | tf_op args[0]
  16.5 1.7 slice_select_fusion.1
  18.3 123.2 %all-reduce.10.cloned.1.call-done = f32[256,256]{0,1:T(8,128)} async-done(((f32[256,256]{0,1:T(8,128)}), f32[256,256]{0,1:T(8,128)}) %all-reduce.10.cloned.1.call-update) | async-done | bytes 262160 | tf_op jit(solution)/shard_map/psum | solution.py:12
  141.5 1.1 copy.8
  142.6 1.0 fusion.27
  143.6 11.7 %cholesky.130 = f32[128,128]{1,0:T(8,128)S(1)} custom-call(f32[128,128]{1,0:T(8,128)S(1)} %cholesky.194), custom_call_target="Cholesky" | custom-call | tf_op jit(solution)/shard_map/jit(cholesky)/cholesky | solution.py:48
  155.3 9.8 %custom-call.13 = f32[1,128,128]{1,2,0:T(8,128)S(1)} custom-call(f32[1,128,128]{2,1,0:T(8,128)S(1)} %get-tuple-element.131), custom_call_target="InvertDiagBlocksLowerTriangular" | custom-call | tf_op jit(solution)/shard_map/jit(cholesky)/cholesky | solution.py:48
  165.7 11.7 %cholesky.147 = f32[128,128]{1,0:T(8,128)S(1)} custom-call(f32[128,128]{1,0:T(8,128)S(1)} %convolution_subtract_fusion.9), custom_call_target="Cholesky" | custom-call | tf_op jit(solution)/shard_map/jit(cholesky)/cholesky | solution.py:48
  177.4 0.6 compare_reduce_fusion.2
  179.5 4.3 while.10
  179.8 0.6 fusion.84
  180.3 1.4 bitcast_dynamic-update-slice_fusion.4
  182.3 1.4 bitcast_dynamic-update-slice_fusion.4
  183.7 19.7 %custom-call.14 = f32[2,128,128]{1,2,0:T(8,128)S(1)} custom-call(f32[2,128,128]{2,1,0:T(8,128)S(1)} %get-tuple-element.92), custom_call_target="InvertDiagBlocksLowerTriangular" | custom-call | tf_op jit(solution)/shard_map/jit(_solve_triangular)/triangular_solve | solution.py:49
  204.7 0.9 copy.19
  205.6 2.5 fusion.8
  208.1 3.2 fusion.7
  211.4 4.9 fusion.2
  216.4 1.8 copy.20
  218.2 5.6 copy.14
  223.8 0.6 compare_reduce_fusion.5
  224.4 35.6 %all-reduce.20.cloned.1.call-done = (f32[1024,256]{0,1:T(8,128)}, f32[512,256]{0,1:T(8,128)}, f32[256,256]{0,1:T(8,128)}) async-done(((f32[1024,256]{0,1:T(8,128)}, f32[512,256]{0,1:T(8,128)}, f32[256,256]{0,1:T(8,128)}), (f32[1024,256]{0,1:T(8,128)}, f32[512,256]{0,1:T(8,128)}, f32[256,256]{0,1:T(8,128)})) %all-reduce.20.cloned.1.call-update) | async-done | bytes 1835024 | tf_op jit(solution)/shard_map/psum | solution.py:12
  260.0 105.8 %all-reduce.12.cloned.1.call-done = f32[2048,256]{0,1:T(8,128)} async-done(((f32[2048,256]{0,1:T(8,128)}), f32[2048,256]{0,1:T(8,128)}) %all-reduce.12.cloned.1.call-update) | async-done | bytes 2097168 | tf_op jit(solution)/shard_map/psum | solution.py:12
  365.7 11.9 %convolution_subtract_fusion.1 = f32[1024,2048]{0,1:T(8,128)S(1)} fusion(f32[1024,2048]{0,1:T(8,128)} %copy.9, f32[1024,256]{0,1:T(8,128)} %get-tuple-element.117, f32[2048,256]{0,1:T(8,128)} %all-reduce.12.cloned.1.call-done), kind=kOutput, calls=%fused_computation.6 | convolution fusion | flops 6444548096 | bytes 19922944 | tf_op jit(solution)/shard_map/dot_general | solution.py:16
  377.6 1.0 fusion.10
  378.7 3.4 copy-done
  382.1 0.7 slice_select_fusion
  382.9 14.4 %convolution_subtract_fusion.3 = f32[512,2048]{0,1:T(8,128)S(1)} fusion(f32[512,2048]{0,1:T(8,128)} %copy.14, f32[512,256]{0,1:T(8,128)S(1)} %copy-done.7, f32[2048,256]{0,1:T(8,128)S(1)} %copy-done.3), kind=kOutput, calls=%fused_computation.8 | convolution fusion | flops 3222274048 | bytes 11010048 | tf_op jit(solution)/shard_map/dot_general | solution.py:16
  397.4 0.7 fusion.19
  398.1 4.8 convolution_subtract_fusion.5
  403.0 2.3 fusion.23
  405.2 101.0 %all-reduce.14.cloned.1.call-done = f32[256,256]{0,1:T(8,128)} async-done(((f32[256,256]{0,1:T(8,128)}), f32[256,256]{0,1:T(8,128)}) %all-reduce.14.cloned.1.call-update) | async-done | bytes 262160 | tf_op jit(solution)/shard_map/psum | solution.py:12
  506.2 1.1 copy.11
  507.2 1.0 fusion.26
  508.2 11.7 %cholesky.164 = f32[128,128]{1,0:T(8,128)S(1)} custom-call(f32[128,128]{1,0:T(8,128)S(1)} %cholesky.197), custom_call_target="Cholesky" | custom-call | tf_op jit(solution)/shard_map/jit(cholesky)/cholesky | solution.py:48
  520.0 9.8 %custom-call.15 = f32[1,128,128]{1,2,0:T(8,128)S(1)} custom-call(f32[1,128,128]{2,1,0:T(8,128)S(1)} %get-tuple-element.127), custom_call_target="InvertDiagBlocksLowerTriangular" | custom-call | tf_op jit(solution)/shard_map/jit(cholesky)/cholesky | solution.py:48
  530.3 11.9 %cholesky.181 = f32[128,128]{1,0:T(8,128)S(1)} custom-call(f32[128,128]{1,0:T(8,128)S(1)} %convolution_subtract_fusion.8), custom_call_target="Cholesky" | custom-call | tf_op jit(solution)/shard_map/jit(cholesky)/cholesky | solution.py:48
  542.3 0.6 compare_reduce_fusion
  542.9 0.6 compare_reduce_fusion.1
  544.8 3.8 while.11
  545.4 1.3 bitcast_dynamic-update-slice_fusion.5
  546.7 0.6 fusion.85
  547.3 1.3 bitcast_dynamic-update-slice_fusion.5
  548.6 19.7 %custom-call.16 = f32[2,128,128]{1,2,0:T(8,128)S(1)} custom-call(f32[2,128,128]{2,1,0:T(8,128)S(1)} %get-tuple-element.93), custom_call_target="InvertDiagBlocksLowerTriangular" | custom-call | tf_op jit(solution)/shard_map/jit(_solve_triangular)/triangular_solve | solution.py:49
  569.2 2.1 convolution_select_fusion.6
  571.3 2.5 convolution_select_fusion.4
  573.8 3.3 fusion.5
  577.2 4.7 fusion
  582.0 43.7 %all-reduce.18.cloned.1.call-done = (f32[1024,256]{0,1:T(8,128)}, f32[512,256]{0,1:T(8,128)}, f32[256,256]{0,1:T(8,128)}) async-done(((f32[1024,256]{0,1:T(8,128)}, f32[512,256]{0,1:T(8,128)}, f32[256,256]{0,1:T(8,128)}), (f32[1024,256]{0,1:T(8,128)}, f32[512,256]{0,1:T(8,128)}, f32[256,256]{0,1:T(8,128)})) %all-reduce.18.cloned.1.call-update) | async-done | bytes 1835024 | tf_op jit(solution)/shard_map/psum | solution.py:12
  625.7 1.8 pad_maximum_fusion
  627.5 0.9 compare_reduce_fusion.4
  628.4 102.3 %all-reduce.16.cloned.1.call-done = f32[2048,256]{1,0:T(8,128)} async-done(((f32[2048,256]{1,0:T(8,128)}), f32[2048,256]{1,0:T(8,128)}) %all-reduce.16.cloned.1.call-update) | async-done | bytes 2097168 | tf_op jit(solution)/shard_map/psum | solution.py:12
  730.8 5.4 convolution_subtract_fusion.4
  736.2 2.3 fusion.24
  738.4 3.0 copy.26
  741.5 6.8 convolution_subtract_fusion.2
  748.3 2.5 fusion.20
  750.8 5.5 copy.25
  756.2 9.8 %convolution_subtract_fusion = f32[1024,2048]{0,1:T(8,128)S(1)} fusion(f32[1024,2048]{0,1:T(8,128)} %copy-done, f32[1024,256]{0,1:T(8,128)S(1)} %copy-done.5, f32[2048,256]{1,0:T(8,128)S(1)} %copy-done.2), kind=kOutput, calls=%fused_computation.5 | convolution fusion | flops 6444548096 | bytes 19922944 | tf_op jit(solution)/shard_map/dot_general | solution.py:16
  766.0 0.9 fusion.11
  766.9 3.8 and_select_fusion
  770.7 9.3 %copy.24 = f32[1024,2048]{1,0:T(8,128)} copy(f32[1024,2048]{0,1:T(8,128)} %and_select_fusion) | data formatting | bytes 16777216
  780.1 26.6 %all-gather.2.cloned.1.call-done = f32[2048,512]{0,1:T(8,128)} async-done(((f32[256,512]{0,1:T(8,128)}), f32[2048,512]{0,1:T(8,128)}) %all-gather.2.cloned.1.call-update) | async-done | bytes 4194320 | tf_op jit(solution)/shard_map/all_gather | solution.py:83
  806.7 4.0 fusion.13
  (79 shorter events, 5.2 us)
Async XLA Ops:
  7.2 134.3 %all-reduce.10.cloned.1.call-start = ((), (), s32[]{:S(2)}) async-start(), calls=%async_computation | async-start | bytes 524288 | tf_op jit(solution)/shard_map/psum | solution.py:12
  18.2 241.8 %all-reduce.20.cloned.1.call-start = ((), (), s32[]{:S(2)}) async-start(), calls=%async_computation.6 | async-start | bytes 3670016 | tf_op jit(solution)/shard_map/psum | solution.py:12
  143.6 60.8 %copy-start.11 = (f32[256,2048]{1,0:T(8,128)S(1)}, f32[256,2048]{1,0:T(8,128)}, u32[]{:S(2)}) copy-start(f32[256,2048]{1,0:T(8,128)} %param.20) | copy-start | bytes 6291460
  211.4 154.4 %all-reduce.12.cloned.1.call-start = ((), (), s32[]{:S(2)}) async-start(), calls=%async_computation.1 | async-start | bytes 4194304 | tf_op jit(solution)/shard_map/psum | solution.py:12
  216.3 289.9 %all-reduce.14.cloned.1.call-start = ((), (), s32[]{:S(2)}) async-start(), calls=%async_computation.2 | async-start | bytes 524288 | tf_op jit(solution)/shard_map/psum | solution.py:12
  365.7 11.9 %copy-start.6 = (f32[1024,256]{0,1:T(8,128)S(1)}, f32[1024,256]{0,1:T(8,128)}, u32[]{:S(2)}) copy-start(f32[1024,256]{0,1:T(8,128)} %get-tuple-element.117) | copy-start | bytes 3145732
  377.6 5.3 copy-start.3
  377.6 5.3 copy-start.7
  378.7 3.4 copy-start
  382.8 242.9 %all-reduce.18.cloned.1.call-start = ((), (), s32[]{:S(2)}) async-start(), calls=%async_computation.5 | async-start | bytes 3670016 | tf_op jit(solution)/shard_map/psum | solution.py:12
  382.9 15.2 %copy-start.4 = (f32[256,2048]{0,1:T(8,128)S(1)}, f32[256,2048]{0,1:T(8,128)}, u32[]{:S(2)}) copy-start(f32[256,2048]{0,1:T(8,128)} %copy.20) | copy-start | bytes 6291460
  382.9 15.2 %copy-start.12 = (f32[256,256]{0,1:T(8,128)S(1)}, f32[256,256]{0,1:T(8,128)}, u32[]{:S(2)}) copy-start(f32[256,256]{0,1:T(8,128)} %get-tuple-element.119) | copy-start | bytes 786436
  398.1 4.9 copy-start.1
  577.1 153.6 %all-reduce.16.cloned.1.call-start = ((), (), s32[]{:S(2)}) async-start(), calls=%async_computation.3 | async-start | bytes 4194304 | tf_op jit(solution)/shard_map/psum | solution.py:12
  581.9 224.7 %all-gather.2.cloned.1.call-start = ((), (), s32[]{:S(2)}) async-start(), calls=%async_computation.4 | async-start | bytes 4718592 | tf_op jit(solution)/shard_map/all_gather | solution.py:83
  628.4 107.8 %copy-start.13 = (f32[256,256]{0,1:T(8,128)S(1)}, f32[256,256]{0,1:T(8,128)}, u32[]{:S(2)}) copy-start(f32[256,256]{0,1:T(8,128)} %get-tuple-element.116) | copy-start | bytes 786436
  738.4 3.0 copy-start.2
  738.4 3.0 copy-start.9
  750.8 5.5 copy-start.5
  770.7 35.9 %copy-start.8 = (f32[512,256]{0,1:T(8,128)S(1)}, f32[512,256]{0,1:T(8,128)}, u32[]{:S(2)}) copy-start(f32[512,256]{0,1:T(8,128)} %get-tuple-element.118) | copy-start | bytes 1572868
  770.7 35.9 %copy-start.10 = (f32[512,256]{0,1:T(8,128)S(1)}, f32[512,256]{0,1:T(8,128)}, u32[]{:S(2)}) copy-start(f32[512,256]{0,1:T(8,128)} %get-tuple-element.115) | copy-start | bytes 1572868
Sparse Core Ops, SparseCore 0:
  18.3 123.1 all-reduce.9
  211.5 48.4 all-reduce.19
  264.2 101.5 all-reduce.11
  383.0 123.1 all-reduce.13
  577.2 48.4 all-reduce.17
  629.2 101.5 all-reduce.15
  733.4 73.2 all-gather.1
where the time goes:
time: 831 us; the launch traced here: 818 us
  waiting for transfers between devices  538 us (65%)
  other arithmetic  129 us (16%)
  matrix products  83.5 us (10%)
  local copies, waits for them, and re-layouts  48.8 us (6%)
  between operations  17.5 us (2%)
    psum x6, waiting for transfers between devices, from_root(): return lax.psum(block, axis)  512 us
    dot_general x15, matrix products, product(): jnp.dot(left, right, precision=lax.Precision.HIGHEST, preferred_element_t...  80.8 us
    another operation x13, other arithmetic, per_device(): factor = jnp.linalg.cholesky(diagonal)  68.7 us
    another operation x5, other arithmetic, per_device(): jax.scipy.linalg.solve_triangular(factor, identity, lower=True)  39.4 us
    unnamed x34, local copies, waits for them, and re-layouts  37.9 us
    all_gather x1, waiting for transfers between devices, per_device(): every_test = lax.all_gather(test_all, 'rows', axis=0, tiled=True)  26.6 us
  transfers between devices with their start and end apart: 7, of which 7 were waited for; matrix products, arithmetic and copies ran while one was open for 11% of the time, Pallas kernels for 0%

commit v1 on v0

--- a/solution.py
+++ b/solution.py
@@ -1,6 +1,8 @@
 import jax
 import jax.numpy as jnp
 from jax import lax
+from jax.experimental import pallas as pl
+from jax.experimental.pallas import tpu as pltpu
 from jax.sharding import PartitionSpec as P
 
 PANEL = 256
@@ -20,7 +22,7 @@
     return state - product(coords, right_rows.T)
 
 
-def per_device(kernel, train_feats, test_feats):
+def general(kernel, train_feats, test_feats):
     blk_rows, blk_cols = kernel.shape
     row_index = lax.axis_index("rows")
     feat_index = lax.axis_index("feat")
@@ -88,9 +90,310 @@
     return (matrix, train_work, test_work, scores)
 
 
+SPAN = NPAN * PANEL
+BASE = 128
+STRIP = 8
+CHUNK = 256
+MESH = pl.DeviceIdType.MESH
+
+
+def exact(left, right, dims):
+    return lax.dot_general(
+        left, right, (dims, ((), ())), precision=lax.Precision.HIGHEST, preferred_element_type=jnp.float32
+    )
+
+
+def base_inverse(block):
+    rows = lax.broadcasted_iota(jnp.int32, (BASE, BASE), 0)
+    lanes = lax.broadcasted_iota(jnp.int32, (BASE, BASE), 1)
+
+    def strip(s, a):
+        alive = rows < BASE - STRIP * s
+        for j in range(STRIP):
+            row = a[j : j + 1, :]
+            scaled = jnp.where(lanes[:1] == j, 1.0, row) / a[j : j + 1, j : j + 1]
+            below = alive & (rows > j)
+            rest = jnp.where(lanes == j, 0.0, a) - a[:, j : j + 1] * scaled
+            a = jnp.where(below, rest, a)
+        a = jnp.concatenate([a[STRIP:], a[:STRIP]], axis=0)
+        return pltpu.roll(a, BASE - STRIP, 1)
+
+    a = lax.fori_loop(0, BASE // STRIP, strip, block)
+    pivots = jnp.sum(jnp.where(rows == lanes, a, 0.0), axis=1, keepdims=True)
+    scale = lax.rsqrt(pivots)
+    scale = scale * (1.5 - 0.5 * pivots * scale * scale)
+    return jnp.where(lanes < rows, a, jnp.where(lanes == rows, 1.0, 0.0)) * scale
+
+
+def factor_step(k, work, inverse):
+    lo, hi = k * BASE, (k + 1) * BASE
+    corner = base_inverse(work[lo:hi, lo:hi])
+    parts = []
+    if k > 0:
+        parts.append(exact(corner, work[lo:hi, :lo], ((1,), (0,))))
+    parts.append(corner)
+    done = jnp.concatenate(parts, axis=1)
+    inverse[lo:hi, :hi] = done
+    if hi < SPAN:
+        inverse[lo:hi, hi:] = jnp.zeros((BASE, SPAN - hi), jnp.float32)
+        left = exact(work[hi:, lo:hi], corner, ((1,), (1,)))
+        ahead = exact(corner, work[lo:hi, hi:], ((1,), (0,)))
+        work[hi:, hi:] = work[hi:, hi:] - exact(left, ahead, ((1,), (0,)))
+        if k > 0:
+            work[hi:, :lo] = work[hi:, :lo] - exact(left, done[:, :lo], ((1,), (0,)))
+        work[hi:, lo:hi] = -exact(left, corner, ((1,), (0,)))
+
+
+def gather_kernel(
+    kernel, train, test, own, cross, winv, work, inverse,
+    own_recv, own_core, own_x, here_recv, there_recv, up_send, down_send, side_send,
+    w_recv, w_core, w_x, w_y, w_z, w_local, local_sem, diag_sem,
+):
+    feat, rows = lax.axis_index("feat"), lax.axis_index("rows")
+    x, c = feat // 2, feat % 2
+    z, y = rows // 2, rows % 2
+    blk, tst, trn = kernel.shape[0], test.shape[0], train.shape[0]
+    n_shared = (blk + tst) // CHUNK
+    n_own = (blk + tst + trn) // CHUNK
+    to_core = {"feat": 2 * x + 1 - c, "rows": rows}
+    to_x = {"feat": lax.rem(feat + 2, 4), "rows": rows}
+    to_y = {"feat": feat, "rows": 2 * z + 1 - y}
+    to_up = {"feat": feat, "rows": jnp.minimum(rows + 2, 6 + y)}
+    to_down = {"feat": feat, "rows": jnp.maximum(rows - 2, y)}
+    has_up, has_down = z < 3, z > 0
+    holder = feat == 0
+    root = holder & (rows == 0)
+    at_source = z == feat
+
+    barrier = pltpu.get_barrier_semaphore()
+
+    def greet(cond, target):
+        @pl.when(cond)
+        def _():
+            pl.semaphore_signal(barrier, inc=1, device_id=target, device_id_type=MESH)
+
+    everyone = ((True, to_core), (c == 0, to_x), (True, to_y), (has_up, to_up), (has_down, to_down))
+    for cond, target in everyone:
+        greet(cond, target)
+    peers = 2 + jnp.where(c == 0, 1, 0) + jnp.where(has_up, 1, 0) + jnp.where(has_down, 1, 0)
+    pl.semaphore_wait(barrier, peers)
+
+    def piece(i):
+        at = i * CHUNK
+        if at < blk:
+            return kernel.at[pl.ds(at, CHUNK), pl.ds(0, SPAN)]
+        if at < blk + tst:
+            return test.at[pl.ds(at - blk, CHUNK), pl.ds(0, SPAN)]
+        return train.at[pl.ds(at - blk - tst, CHUNK), pl.ds(0, SPAN)]
+
+    def own_at(i):
+        return own.at[pl.ds(i * CHUNK, CHUNK), :]
+
+    def cross_at(side, i):
+        return cross.at[side, pl.ds(i * CHUNK, CHUNK), :]
+
+    def send(src, dst, sent, received, target):
+        return pltpu.make_async_remote_copy(
+            src_ref=src, dst_ref=dst, send_sem=sent, recv_sem=received, device_id=target, device_id_type=MESH
+        )
+
+    def spread(src, i):
+        @pl.when(has_up & (z >= feat))
+        def _():
+            send(src, cross_at(y, i), up_send.at[i], here_recv.at[i], to_up).start()
+
+        @pl.when(has_down & (z <= feat))
+        def _():
+            send(src, cross_at(y, i), down_send.at[i], here_recv.at[i], to_down).start()
+
+        send(src, cross_at(y, i), side_send.at[i], there_recv.at[i], to_y).start()
+
+    diag = pltpu.make_async_copy(kernel.at[pl.ds(0, SPAN), pl.ds(0, SPAN)], work, diag_sem)
+
+    @pl.when(root)
+    def _():
+        diag.start()
+
+    @pl.when(holder)
+    def _():
+        for i in range(n_own):
+            send(piece(i), own_at(i), own_x.at[i], own_recv.at[i], to_x).start()
+            send(piece(i), own_at(i), own_core.at[i], own_recv.at[i], to_core).start()
+            if i < n_shared:
+                @pl.when(at_source)
+                def _():
+                    spread(piece(i), i)
+
+        for i in range(n_own):
+            pltpu.make_async_copy(piece(i), own_at(i), local_sem.at[i]).start()
+
+    def w_at(k):
+        return winv.at[pl.ds(k * BASE, BASE), :]
+
+    def w_sends(k, src):
+        rows_k = w_at(k)
+        return (
+            (holder & (y == 0) & has_up, send(src, rows_k, w_z.at[k], w_recv.at[k], to_up)),
+            (holder & (y == 0), send(src, rows_k, w_y.at[k], w_recv.at[k], to_y)),
+            (holder, send(src, rows_k, w_x.at[k], w_recv.at[k], to_x)),
+            (c == 0, send(src, rows_k, w_core.at[k], w_recv.at[k], to_core)),
+        )
+
+    @pl.when(root)
+    def _():
+        diag.wait()
+        for k in range(SPAN // BASE):
+            factor_step(k, work, inverse)
+            src = inverse.at[pl.ds(k * BASE, BASE), :]
+            for cond, copy in w_sends(k, src):
+                @pl.when(cond)
+                def _():
+                    copy.start()
+            pltpu.make_async_copy(src, w_at(k), w_local.at[k]).start()
+
+    for i in range(n_own):
+        @pl.when(feat != 0)
+        def _():
+            send(own_at(i), own_at(i), own_x.at[i], own_recv.at[i], to_core).wait_recv()
+
+        @pl.when(feat == 2)
+        def _():
+            send(own_at(i), own_at(i), own_core.at[i], own_recv.at[i], to_core).start()
+
+        if i < n_shared:
+            @pl.when(at_source & (feat != 0))
+            def _():
+                spread(own_at(i), i)
+
+            @pl.when(jnp.logical_not(at_source))
+            def _():
+                send(cross_at(y, i), cross_at(y, i), side_send.at[i], here_recv.at[i], to_y).wait_recv()
+                spread(cross_at(y, i), i)
+
+    @pl.when(holder)
+    def _():
+        for i in range(n_own):
+            pltpu.make_async_copy(piece(i), own_at(i), local_sem.at[i]).wait()
+
+    @pl.when(at_source)
+    def _():
+        for i in range(n_shared):
+            pltpu.make_async_copy(own_at(i), cross_at(y, i), here_recv.at[i]).start()
+
+    for k in range(SPAN // BASE):
+        @pl.when(jnp.logical_not(root))
+        def _():
+            send(w_at(k), w_at(k), w_core.at[k], w_recv.at[k], to_core).wait_recv()
+            for cond, copy in w_sends(k, w_at(k)):
+                @pl.when(cond)
+                def _():
+                    copy.start()
+
+    for k in range(SPAN // BASE):
+        for cond, copy in w_sends(k, w_at(k)):
+            @pl.when(cond)
+            def _():
+                copy.wait_send()
+
+        @pl.when(root)
+        def _():
+            pltpu.make_async_copy(w_at(k), w_at(k), w_local.at[k]).wait()
+
+    for i in range(n_own):
+        @pl.when(holder)
+        def _():
+            send(own_at(i), own_at(i), own_x.at[i], own_recv.at[i], to_x).wait_send()
+
+        @pl.when(c == 0)
+        def _():
+            send(own_at(i), own_at(i), own_core.at[i], own_recv.at[i], to_core).wait_send()
+
+    for i in range(n_shared):
+        @pl.when(at_source)
+        def _():
+            pltpu.make_async_copy(own_at(i), cross_at(y, i), here_recv.at[i]).wait()
+
+        @pl.when(has_up & (z >= feat))
+        def _():
+            send(own_at(i), cross_at(y, i), up_send.at[i], here_recv.at[i], to_up).wait_send()
+
+        @pl.when(has_down & (z <= feat))
+        def _():
+            send(own_at(i), cross_at(y, i), down_send.at[i], here_recv.at[i], to_down).wait_send()
+
+        side = send(own_at(i), cross_at(1 - y, i), side_send.at[i], there_recv.at[i], to_y)
+        side.wait_send()
+        side.wait_recv()
+
+
+def gather(kernel, train, test):
+    blk, tst, trn = kernel.shape[0], test.shape[0], train.shape[0]
+    n_shared = (blk + tst) // CHUNK
+    n_own = (blk + tst + trn) // CHUNK
+    n_w = SPAN // BASE
+    dma = pltpu.SemaphoreType.DMA
+    anywhere = pl.BlockSpec(memory_space=pl.ANY)
+    return pl.pallas_call(
+        gather_kernel,
+        out_shape=(
+            jax.ShapeDtypeStruct((blk + tst + trn, SPAN), jnp.float32),
+            jax.ShapeDtypeStruct((2, blk + tst, SPAN), jnp.float32),
+            jax.ShapeDtypeStruct((SPAN, SPAN), jnp.float32),
+        ),
+        in_specs=[anywhere] * 3,
+        out_specs=(anywhere,) * 3,
+        scratch_shapes=[
+            pltpu.VMEM((SPAN, SPAN), jnp.float32),
+            pltpu.VMEM((SPAN, SPAN), jnp.float32),
+            dma((n_own,)), dma((n_own,)), dma((n_own,)),
+            dma((n_shared,)), dma((n_shared,)), dma((n_shared,)), dma((n_shared,)), dma((n_shared,)),
+            dma((n_w,)), dma((n_w,)), dma((n_w,)), dma((n_w,)), dma((n_w,)), dma((n_w,)),
+            dma((n_own,)), dma,
+        ],
+        compiler_params=pltpu.CompilerParams(
+            collective_id=0, has_side_effects=True, vmem_limit_bytes=24 * 1024 * 1024
+        ),
+    )(kernel, train, test)
+
+
+def fast(left, right):
+    return lax.dot_general(
+        left, right, (((1,), (1,)), ((), ())), precision=lax.Precision.HIGH, preferred_element_type=jnp.float32
+    )
+
+
+def per_device(kernel, train_feats, test_feats):
+    blk, blk_cols = kernel.shape
+    tst, trn = test_feats.shape[0], train_feats.shape[0]
+    row_ids = lax.axis_index("rows") * blk + lax.broadcasted_iota(jnp.int32, (blk, 1), 0)
+    col_ids = lax.axis_index("feat") * blk_cols + lax.broadcasted_iota(jnp.int32, (1, blk_cols), 1)
+    own, cross, winv = gather(kernel, train_feats, test_feats)
+    coords = fast(own, winv)
+    panel_of = (jnp.arange(SPAN, dtype=jnp.int32) // PANEL) * PANEL
+    left = jnp.where(row_ids >= panel_of[None, :], coords[:blk], 0.0)
+    test_coords, train_coords = coords[blk : blk + tst], coords[blk + tst :]
+    other = fast(cross.reshape(2 * (blk + tst), SPAN), winv).reshape(2, blk + tst, SPAN)
+    right = other[:, :blk].reshape(2 * blk, SPAN)
+    scored = other[:, blk:].reshape(2 * tst, SPAN)
+
+    def updated(state, part):
+        rest = state - fast(part, right)
+        padded = jnp.pad(part, ((0, 0), (0, blk_cols - SPAN)))
+        return jnp.where(col_ids < SPAN, padded, rest)
+
+    matrix = jnp.where((row_ids < SPAN) & (col_ids >= SPAN), 0.0, updated(kernel, left))
+    return (
+        matrix,
+        updated(train_feats, train_coords),
+        updated(test_feats, test_coords),
+        fast(train_coords, scored),
+    )
+
+
 def solution(mesh):
+    wide = mesh.shape["feat"] == 4 and mesh.shape["rows"] == 8
     return jax.shard_map(
-        per_device,
+        per_device if wide else general,
         mesh=mesh,
         in_specs=(P("rows", "feat"), P("rows", "feat"), P("rows", "feat")),
         out_specs=(P("rows", "feat"), P("rows", "feat"), P("rows", "feat"), P("rows", "feat")),

time: 831 us -> 138 us (0.17); the launches traced: 818 us -> 138 us
  waiting for transfers between devices: 538 us -> 0 us
  other arithmetic: 129 us -> 0.24 us
  Pallas kernels: 0 us -> 102 us
  matrix products: 83.5 us -> 27.3 us
  local copies, waits for them, and re-layouts: 48.8 us -> 7.73 us
  between operations: 17.5 us -> 0.76 us
    psum x6 -> x0, waiting for transfers between devices: 512 us -> none  [from_root(): return lax.psum(block, axis)]
    another operation x20 -> x0, other arithmetic: 110 us -> none  [the longest x13 68.7 us: per_device(): factor = jnp.linalg.cholesky(diagonal)]
    pallas_call x0 -> x1, Pallas kernels: none -> 102 us  [gather(): pl.pallas_call(gather_kernel, out_shape=(jax.ShapeDtypeStruct((blk + tst...]
    dot_general x15 -> x6, matrix products: 80.8 us -> 27.3 us  [fast(): lax.dot_general(left, right, (((1,), (1,)), ((), ())), precision=lax.Prec...]
    unnamed x34 -> x12, local copies, waits for them, and re-layouts: 37.9 us -> 7.17 us
    all_gather x1 -> x0, waiting for transfers between devices: 26.6 us -> none  [per_device(): every_test = lax.all_gather(test_all, 'rows', axis=0, tiled=True)]
    scatter x6 -> x0, other arithmetic: 9.66 us -> none  [the longest x2 4.51 us: per_device(): test_work.at[:, first_col:last_col]]
  transfers between devices with their start and end apart: 7 -> 0, of which waited for: 7 -> 0; matrix products, arithmetic and copies ran while one was open for 11% -> 0% of each run, Pallas kernels for 0% -> 0%
where the time goes in v1:
time: 138 us
  Pallas kernels  102 us (74%)
  matrix products  27.3 us (20%)
  local copies, waits for them, and re-layouts  7.73 us (6%)
    pallas_call x1, Pallas kernels, gather(): pl.pallas_call(gather_kernel, out_shape=(jax.ShapeDtypeStruct((blk + tst...  102 us
    dot_general x6, matrix products, fast(): lax.dot_general(left, right, (((1,), (1,)), ((), ())), precision=lax.Prec...  27.3 us
    unnamed x12, local copies, waits for them, and re-layouts  7.17 us

profile of v1, /device:TPU:31, one launch (start us, length us, event | category | flops | bytes accessed | tf_op | source)
XLA Modules:
  0.0 138.1 jit_solution(7068131967018835209)
XLA Ops:
  0.7 0.0 copy-start
  0.7 3.4 %copy-done = f32[1024,2048]{1,0:T(8,128)S(1)} copy-done((f32[1024,2048]{1,0:T(8,128)S(1)}, f32[1024,2048]{1,0:T(8,128)}, u32[]{:S(2)}) %copy-start) | copy-done | bytes 8388632
  4.1 0.0 copy-start.1
  4.1 2.2 %copy-done.1 = f32[512,2048]{1,0:T(8,128)S(1)} copy-done((f32[512,2048]{1,0:T(8,128)S(1)}, f32[512,2048]{1,0:T(8,128)}, u32[]{:S(2)}) %copy-start.1) | copy-done | bytes 4194328
  6.3 0.0 copy-start.2
  6.3 1.6 %copy-done.2 = f32[256,2048]{1,0:T(8,128)S(1)} copy-done((f32[256,2048]{1,0:T(8,128)S(1)}, f32[256,2048]{1,0:T(8,128)}, u32[]{:S(2)}) %copy-start.2) | copy-done | bytes 2097176
  7.9 102.1 %shard_map.66 = (f32[1792,512]{1,0:T(8,128)S(1)}, f32[2,1280,512]{2,1,0:T(8,128)S(1)}, f32[512,512]{1,0:T(8,128)S(1)}) custom-call(f32[1024,2048]{1,0:T(8,128)S(1)} %copy-done, f32[512,2048]{1,0:T(8,128)S(1)} %copy-done.1, f32[256,2048]{1,0:T(8,128)S(1)} %copy-done.2), custom_call_target="tpu_custom_call" | custom-call | tf_op jit(solution)/shard_map/pallas_call | solution.py:336
  110.0 3.1 %fusion.11 = f32[1792,512]{1,0:T(8,128)S(1)} fusion(f32[1792,512]{1,0:T(8,128)S(1)} %get-tuple-element.7, f32[512,512]{1,0:T(8,128)S(1)} %get-tuple-element.8), kind=kOutput, calls=%fused_computation.22 | convolution fusion | flops 2818572288 | bytes 8388608 | tf_op jit(solution)/shard_map/dot_general | solution.py:360
  113.1 0.0 copy-start.3
  113.1 4.3 %fusion.1 = f32[2,1280,512]{2,1,0:T(8,128)S(1)} fusion(f32[2,1280,512]{2,1,0:T(8,128)S(1)} %get-tuple-element.9, f32[512,512]{1,0:T(8,128)S(1)} %get-tuple-element.8), kind=kOutput, calls=%fused_computation.5 | convolution fusion | flops 4026531840 | bytes 11534336 | tf_op jit(solution)/shard_map/dot_general | solution.py:360
  117.4 0.1 slice.24
  117.5 0.4 slice.21
  117.9 2.0 %fusion.9 = f32[512,512]{1,0:T(8,128)} fusion(f32[512,512]{1,0:T(8,128)S(1)} %bitcast.20, f32[1792,512]{1,0:T(8,128)S(1)} %fusion.11), kind=kOutput, calls=%fused_computation.20 | convolution fusion | flops 805306368 | bytes 3145728 | tf_op jit(solution)/shard_map/dot_general | solution.py:360
  119.9 0.0 copy-done.3
  119.9 0.2 slice_select_fusion
  120.2 0.0 slice-start.2
  120.2 0.0 slice-start
  120.2 3.2 %fusion = f32[256,2048]{1,0:T(8,128)} fusion(f32[256,2048]{1,0:T(8,128)S(1)} %copy-done.2, f32[256,512]{1,0:T(8,128)S(1)} %slice.23, f32[2048,512]{1,0:T(8,128)S(1)} %bitcast.17, pred[2048]{0:T(1024)(128)(4,1)S(1)} %get-tuple-element.10), kind=kOutput, calls=%fused_computation.3 | convolution fusion | flops 1611661312 | bytes 8914944 | tf_op jit(solution)/shard_map/dot_general | solution.py:360
  123.4 0.0 slice-done.2
  123.4 0.0 slice-start.1
  123.4 5.1 %subtract_select_fusion = f32[512,2048]{1,0:T(8,128)} fusion(f32[512,2048]{1,0:T(8,128)S(1)} %copy-done.1, f32[512,512]{1,0:T(8,128)S(1)} %slice-done.2, f32[2048,512]{1,0:T(8,128)S(1)} %bitcast.18, pred[2048]{0:T(1024)(128)(4,1)S(1)} %get-tuple-element.10), kind=kOutput, calls=%fused_computation.1 | convolution fusion | flops 3223322624 | bytes 13633536 | tf_op jit(solution)/shard_map/dot_general | solution.py:360
  128.5 0.0 slice-done
  128.5 0.0 slice-done.1
  128.6 9.6 %select_select_fusion = f32[1024,2048]{1,0:T(8,128)} fusion(f32[1024,2048]{1,0:T(8,128)S(1)} %bitcast.16, f32[1024,512]{1,0:T(8,128)S(1)} %slice_select_fusion, pred[2048]{0:T(1024)(128)(4,1)S(1)} %get-tuple-element.10, pred[2048]{0:T(1024)(128)(4,1)S(1)} %get-tuple-element.11, pred[1024]{0:T(1024)(128)(4,1)S(1)} %broadcast_compare_fusion, ...), kind=kOutput, calls=%fused_computation | convolution fusion | flops 6450839552 | bytes 23073792 | tf_op jit(solution)/shard_map/dot_general | solution.py:360
  (6 shorter events, 0.1 us)
Async XLA Ops:
  0.7 3.4 %copy-start = (f32[1024,2048]{1,0:T(8,128)S(1)}, f32[1024,2048]{1,0:T(8,128)}, u32[]{:S(2)}) copy-start(f32[1024,2048]{1,0:T(8,128)} %kernel.1) | copy-start | bytes 25165828
  4.1 2.2 %copy-start.1 = (f32[512,2048]{1,0:T(8,128)S(1)}, f32[512,2048]{1,0:T(8,128)}, u32[]{:S(2)}) copy-start(f32[512,2048]{1,0:T(8,128)} %train.1) | copy-start | bytes 12582916
  6.3 1.6 %copy-start.2 = (f32[256,2048]{1,0:T(8,128)S(1)}, f32[256,2048]{1,0:T(8,128)}, u32[]{:S(2)}) copy-start(f32[256,2048]{1,0:T(8,128)} %test.1) | copy-start | bytes 6291460
  113.1 6.9 %copy-start.3 = (f32[1792,512]{1,0:T(8,128)}, f32[1792,512]{1,0:T(8,128)S(1)}, u32[]{:S(2)}) copy-start(f32[1792,512]{1,0:T(8,128)S(1)} %fusion.11) | copy-start | bytes 11010052
  120.2 3.3 %slice-start.2 = ((f32[1792,512]{1,0:T(8,128)}), f32[512,512]{1,0:T(8,128)S(1)}, s32[]{:S(2)}) async-start(f32[1792,512]{1,0:T(8,128)} %copy-done.3), calls=%async_computation.2 | async-start | bytes 2097152 | tf_op jit(solution)/shard_map/slice | solution.py:374
  120.2 8.4 %slice-start = ((s8[8388608]{0:T(1024)(128)(4,1)}), s8[4194304]{0:T(1024)(128)(4,1)S(1)}, s32[]{:S(2)}) async-start(s8[8388608]{0:T(1024)(128)(4,1)} %bitcast.15), calls=%async_computation | async-start | bytes 8388608
  123.4 5.1 %slice-start.1 = ((s8[8388608]{0:T(1024)(128)(4,1)}), s8[4194304]{0:T(1024)(128)(4,1)S(1)}, s32[]{:S(2)}) async-start(s8[8388608]{0:T(1024)(128)(4,1)} %bitcast.15), calls=%async_computation.1 | async-start | bytes 8388608

commit v2 on v1

--- a/solution.py
+++ b/solution.py
@@ -94,6 +94,7 @@
 BASE = 128
 STRIP = 8
 CHUNK = 256
+PIECE = 64
 MESH = pl.DeviceIdType.MESH
 
 
@@ -228,7 +229,7 @@
             pltpu.make_async_copy(piece(i), own_at(i), local_sem.at[i]).start()
 
     def w_at(k):
-        return winv.at[pl.ds(k * BASE, BASE), :]
+        return winv.at[pl.ds(k * PIECE, PIECE), :]
 
     def w_sends(k, src):
         rows_k = w_at(k)
@@ -244,12 +245,13 @@
         diag.wait()
         for k in range(SPAN // BASE):
             factor_step(k, work, inverse)
-            src = inverse.at[pl.ds(k * BASE, BASE), :]
-            for cond, copy in w_sends(k, src):
-                @pl.when(cond)
-                def _():
-                    copy.start()
-            pltpu.make_async_copy(src, w_at(k), w_local.at[k]).start()
+            for part in range(k * BASE // PIECE, (k + 1) * BASE // PIECE):
+                src = inverse.at[pl.ds(part * PIECE, PIECE), :]
+                for cond, copy in w_sends(part, src):
+                    @pl.when(cond)
+                    def _():
+                        copy.start()
+                pltpu.make_async_copy(src, w_at(part), w_local.at[part]).start()
 
     for i in range(n_own):
         @pl.when(feat != 0)
@@ -280,7 +282,7 @@
         for i in range(n_shared):
             pltpu.make_async_copy(own_at(i), cross_at(y, i), here_recv.at[i]).start()
 
-    for k in range(SPAN // BASE):
+    for k in range(SPAN // PIECE):
         @pl.when(jnp.logical_not(root))
         def _():
             send(w_at(k), w_at(k), w_core.at[k], w_recv.at[k], to_core).wait_recv()
@@ -289,7 +291,7 @@
                 def _():
                     copy.start()
 
-    for k in range(SPAN // BASE):
+    for k in range(SPAN // PIECE):
         for cond, copy in w_sends(k, w_at(k)):
             @pl.when(cond)
             def _():
@@ -330,7 +332,7 @@
     blk, tst, trn = kernel.shape[0], test.shape[0], train.shape[0]
     n_shared = (blk + tst) // CHUNK
     n_own = (blk + tst + trn) // CHUNK
-    n_w = SPAN // BASE
+    n_w = SPAN // PIECE
     dma = pltpu.SemaphoreType.DMA
     anywhere = pl.BlockSpec(memory_space=pl.ANY)
     return pl.pallas_call(
@@ -351,7 +353,7 @@
             dma((n_own,)), dma,
         ],
         compiler_params=pltpu.CompilerParams(
-            collective_id=0, has_side_effects=True, vmem_limit_bytes=24 * 1024 * 1024
+            collective_id=0, has_side_effects=True, vmem_limit_bytes=44 * 1024 * 1024
         ),
     )(kernel, train, test)
 

time: 138 us -> 134 us (0.971)
  local copies, waits for them, and re-layouts: 7.73 us -> 2.17 us
    unnamed x12, local copies, waits for them, and re-layouts: 7.17 us -> 1.61 us
where the time goes in v2:
time: 134 us
  Pallas kernels  103 us (77%)
  matrix products  27.7 us (21%)
  local copies, waits for them, and re-layouts  2.17 us (2%)
    pallas_call x1, Pallas kernels, gather(): pl.pallas_call(gather_kernel, out_shape=(jax.ShapeDtypeStruct((blk + tst...  103 us
    dot_general x6, matrix products, fast(): lax.dot_general(left, right, (((1,), (1,)), ((), ())), precision=lax.Prec...  27.7 us

profile of v2, /device:TPU:31, one launch (start us, length us, event | category | flops | bytes accessed | tf_op | source)
XLA Modules:
  0.0 134.3 jit_solution(1106842298809789546)
XLA Ops:
  0.7 0.0 copy-start
  0.7 1.6 %copy-done = f32[256,2048]{1,0:T(8,128)S(1)} copy-done((f32[256,2048]{1,0:T(8,128)S(1)}, f32[256,2048]{1,0:T(8,128)}, u32[]{:S(2)}) %copy-start) | copy-done | bytes 2097176
  2.3 103.4 %shard_map.66 = (f32[1792,512]{1,0:T(8,128)S(1)}, f32[2,1280,512]{2,1,0:T(8,128)}, f32[512,512]{1,0:T(8,128)S(1)}) custom-call(f32[1024,2048]{1,0:T(8,128)} %kernel.1, f32[512,2048]{1,0:T(8,128)} %train.1, f32[256,2048]{1,0:T(8,128)S(1)} %copy-done), custom_call_target="tpu_custom_call" | custom-call | tf_op jit(solution)/shard_map/pallas_call | solution.py:338
  105.7 0.0 copy-start.1
  105.7 3.1 %fusion.11 = f32[1792,512]{1,0:T(8,128)S(1)} fusion(f32[1792,512]{1,0:T(8,128)S(1)} %get-tuple-element.7, f32[512,512]{1,0:T(8,128)S(1)} %get-tuple-element.8), kind=kOutput, calls=%fused_computation.22 | convolution fusion | flops 2818572288 | bytes 8388608 | tf_op jit(solution)/shard_map/dot_general | solution.py:362
  108.8 0.0 copy-done.1
  108.8 0.0 copy-start.2
  108.8 4.3 %fusion.1 = f32[2,1280,512]{2,1,0:T(8,128)S(1)} fusion(f32[2,1280,512]{2,1,0:T(8,128)S(1)} %copy-done.1, f32[512,512]{1,0:T(8,128)S(1)} %get-tuple-element.8), kind=kOutput, calls=%fused_computation.5 | convolution fusion | flops 4026531840 | bytes 11534336 | tf_op jit(solution)/shard_map/dot_general | solution.py:362
  113.1 0.1 slice.24
  113.2 0.4 slice.21
  113.7 2.0 %fusion.9 = f32[512,512]{1,0:T(8,128)} fusion(f32[512,512]{1,0:T(8,128)S(1)} %bitcast.20, f32[1792,512]{1,0:T(8,128)S(1)} %fusion.11), kind=kOutput, calls=%fused_computation.20 | convolution fusion | flops 805306368 | bytes 3145728 | tf_op jit(solution)/shard_map/dot_general | solution.py:362
  115.7 0.0 copy-done.2
  115.7 0.0 copy-start.3
  115.7 0.2 slice_select_fusion
  115.9 0.0 slice-start.2
  115.9 0.0 slice-start
  115.9 3.2 %fusion = f32[256,2048]{1,0:T(8,128)} fusion(f32[256,2048]{1,0:T(8,128)S(1)} %copy-done, f32[256,512]{1,0:T(8,128)S(1)} %slice.23, f32[2048,512]{1,0:T(8,128)S(1)} %bitcast.15, pred[2048]{0:T(1024)(128)(4,1)S(1)} %get-tuple-element.10), kind=kOutput, calls=%fused_computation.3 | convolution fusion | flops 1611661312 | bytes 8914944 | tf_op jit(solution)/shard_map/dot_general | solution.py:362
  119.2 0.0 copy-done.3
  119.2 0.0 slice-done.2
  119.2 0.0 slice-start.1
  119.2 5.6 %subtract_select_fusion = f32[512,2048]{1,0:T(8,128)} fusion(f32[512,2048]{1,0:T(8,128)S(1)} %copy-done.3, f32[512,512]{1,0:T(8,128)S(1)} %slice-done.2, f32[2048,512]{1,0:T(8,128)S(1)} %bitcast.16, pred[2048]{0:T(1024)(128)(4,1)S(1)} %get-tuple-element.10), kind=kOutput, calls=%fused_computation.1 | convolution fusion | flops 3223322624 | bytes 13633536 | tf_op jit(solution)/shard_map/dot_general | solution.py:362
  124.7 0.0 slice-done
  124.7 0.0 slice-done.1
  124.7 9.6 %select_select_fusion = f32[1024,2048]{1,0:T(8,128)} fusion(f32[1024,2048]{1,0:T(8,128)S(1)} %bitcast.19, f32[1024,512]{1,0:T(8,128)S(1)} %slice_select_fusion, pred[2048]{0:T(1024)(128)(4,1)S(1)} %get-tuple-element.10, pred[2048]{0:T(1024)(128)(4,1)S(1)} %get-tuple-element.11, pred[1024]{0:T(1024)(128)(4,1)S(1)} %broadcast_compare_fusion, ...), kind=kOutput, calls=%fused_computation | convolution fusion | flops 6450839552 | bytes 23073792 | tf_op jit(solution)/shard_map/dot_general | solution.py:362
  (6 shorter events, 0.1 us)
Async XLA Ops:
  0.7 1.6 %copy-start = (f32[256,2048]{1,0:T(8,128)S(1)}, f32[256,2048]{1,0:T(8,128)}, u32[]{:S(2)}) copy-start(f32[256,2048]{1,0:T(8,128)} %test.1) | copy-start | bytes 6291460
  105.7 3.1 %copy-start.1 = (f32[2,1280,512]{2,1,0:T(8,128)S(1)}, f32[2,1280,512]{2,1,0:T(8,128)}, u32[]{:S(2)}) copy-start(f32[2,1280,512]{2,1,0:T(8,128)} %get-tuple-element.9) | copy-start | bytes 15728644
  108.8 6.9 %copy-start.2 = (f32[1792,512]{1,0:T(8,128)}, f32[1792,512]{1,0:T(8,128)S(1)}, u32[]{:S(2)}) copy-start(f32[1792,512]{1,0:T(8,128)S(1)} %fusion.11) | copy-start | bytes 11010052
  115.7 3.5 %copy-start.3 = (f32[512,2048]{1,0:T(8,128)S(1)}, f32[512,2048]{1,0:T(8,128)}, u32[]{:S(2)}) copy-start(f32[512,2048]{1,0:T(8,128)} %train.1) | copy-start | bytes 12582916
  115.9 3.3 %slice-start.2 = ((f32[1792,512]{1,0:T(8,128)}), f32[512,512]{1,0:T(8,128)S(1)}, s32[]{:S(2)}) async-start(f32[1792,512]{1,0:T(8,128)} %copy-done.2), calls=%async_computation.2 | async-start | bytes 2097152 | tf_op jit(solution)/shard_map/slice | solution.py:376
  115.9 8.8 %slice-start = ((s8[8388608]{0:T(1024)(128)(4,1)}), s8[4194304]{0:T(1024)(128)(4,1)S(1)}, s32[]{:S(2)}) async-start(s8[8388608]{0:T(1024)(128)(4,1)} %bitcast.18), calls=%async_computation | async-start | bytes 8388608
  119.2 5.6 %slice-start.1 = ((s8[8388608]{0:T(1024)(128)(4,1)}), s8[4194304]{0:T(1024)(128)(4,1)S(1)}, s32[]{:S(2)}) async-start(s8[8388608]{0:T(1024)(128)(4,1)} %bitcast.18), calls=%async_computation.1 | async-start | bytes 8388608

commit v3 on v2

--- a/solution.py
+++ b/solution.py
@@ -253,36 +253,7 @@
                         copy.start()
                 pltpu.make_async_copy(src, w_at(part), w_local.at[part]).start()
 
-    for i in range(n_own):
-        @pl.when(feat != 0)
-        def _():
-            send(own_at(i), own_at(i), own_x.at[i], own_recv.at[i], to_core).wait_recv()
-
-        @pl.when(feat == 2)
-        def _():
-            send(own_at(i), own_at(i), own_core.at[i], own_recv.at[i], to_core).start()
-
-        if i < n_shared:
-            @pl.when(at_source & (feat != 0))
-            def _():
-                spread(own_at(i), i)
-
-            @pl.when(jnp.logical_not(at_source))
-            def _():
-                send(cross_at(y, i), cross_at(y, i), side_send.at[i], here_recv.at[i], to_y).wait_recv()
-                spread(cross_at(y, i), i)
-
-    @pl.when(holder)
-    def _():
-        for i in range(n_own):
-            pltpu.make_async_copy(piece(i), own_at(i), local_sem.at[i]).wait()
-
-    @pl.when(at_source)
-    def _():
-        for i in range(n_shared):
-            pltpu.make_async_copy(own_at(i), cross_at(y, i), here_recv.at[i]).start()
-
-    for k in range(SPAN // PIECE):
+    def relay(k):
         @pl.when(jnp.logical_not(root))
         def _():
             send(w_at(k), w_at(k), w_core.at[k], w_recv.at[k], to_core).wait_recv()
@@ -290,6 +261,42 @@
                 @pl.when(cond)
                 def _():
                     copy.start()
+
+    for i in range(n_own):
+        if 2 <= i <= 4:
+            for k in range((i - 2) * BASE // PIECE, (i - 1) * BASE // PIECE):
+                relay(k)
+
+        @pl.when(feat != 0)
+        def _():
+            send(own_at(i), own_at(i), own_x.at[i], own_recv.at[i], to_core).wait_recv()
+
+        @pl.when(feat == 2)
+        def _():
+            send(own_at(i), own_at(i), own_core.at[i], own_recv.at[i], to_core).start()
+
+        if i < n_shared:
+            @pl.when(at_source & (feat != 0))
+            def _():
+                spread(own_at(i), i)
+
+            @pl.when(jnp.logical_not(at_source))
+            def _():
+                send(cross_at(y, i), cross_at(y, i), side_send.at[i], here_recv.at[i], to_y).wait_recv()
+                spread(cross_at(y, i), i)
+
+    @pl.when(holder)
+    def _():
+        for i in range(n_own):
+            pltpu.make_async_copy(piece(i), own_at(i), local_sem.at[i]).wait()
+
+    @pl.when(at_source)
+    def _():
+        for i in range(n_shared):
+            pltpu.make_async_copy(own_at(i), cross_at(y, i), here_recv.at[i]).start()
+
+    for k in range(3 * BASE // PIECE, SPAN // PIECE):
+        relay(k)
 
     for k in range(SPAN // PIECE):
         for cond, copy in w_sends(k, w_at(k)):

time: 134 us -> 161 us (1.20)
  the two profiles are of different devices: /device:TPU:31 before, /device:TPU:3 now
where the time goes in v3:
time: 161 us
  Pallas kernels  130 us (81%)
  matrix products  27.7 us (17%)
  local copies, waits for them, and re-layouts  2.17 us (1%)
    pallas_call x1, Pallas kernels, gather(): pl.pallas_call(gather_kernel, out_shape=(jax.ShapeDtypeStruct((blk + tst...  130 us
    dot_general x6, matrix products, fast(): lax.dot_general(left, right, (((1,), (1,)), ((), ())), precision=lax.Prec...  27.7 us

profile of v3, /device:TPU:3, one launch (start us, length us, event | category | flops | bytes accessed | tf_op | source)
XLA Modules:
  0.0 161.2 jit_solution(16114187749827879401)
XLA Ops:
  0.7 0.0 copy-start
  0.7 1.6 copy-done
  2.3 130.3 %shard_map.66 = (f32[1792,512]{1,0:T(8,128)S(1)}, f32[2,1280,512]{2,1,0:T(8,128)}, f32[512,512]{1,0:T(8,128)S(1)}) custom-call(f32[1024,2048]{1,0:T(8,128)} %kernel.1, f32[512,2048]{1,0:T(8,128)} %train.1, f32[256,2048]{1,0:T(8,128)S(1)} %copy-done), custom_call_target="tpu_custom_call" | custom-call | tf_op jit(solution)/shard_map/pallas_call | solution.py:345
  132.6 0.0 copy-start.1
  132.6 3.1 %fusion.11 = f32[1792,512]{1,0:T(8,128)S(1)} fusion(f32[1792,512]{1,0:T(8,128)S(1)} %get-tuple-element.7, f32[512,512]{1,0:T(8,128)S(1)} %get-tuple-element.8), kind=kOutput, calls=%fused_computation.22 | convolution fusion | flops 2818572288 | bytes 8388608 | tf_op jit(solution)/shard_map/dot_general | solution.py:369
  135.7 0.0 copy-done.1
  135.7 0.0 copy-start.2
  135.7 4.3 %fusion.1 = f32[2,1280,512]{2,1,0:T(8,128)S(1)} fusion(f32[2,1280,512]{2,1,0:T(8,128)S(1)} %copy-done.1, f32[512,512]{1,0:T(8,128)S(1)} %get-tuple-element.8), kind=kOutput, calls=%fused_computation.5 | convolution fusion | flops 4026531840 | bytes 11534336 | tf_op jit(solution)/shard_map/dot_general | solution.py:369
  140.0 0.1 slice.24
  140.1 0.4 slice.21
  140.6 2.0 %fusion.9 = f32[512,512]{1,0:T(8,128)} fusion(f32[512,512]{1,0:T(8,128)S(1)} %bitcast.20, f32[1792,512]{1,0:T(8,128)S(1)} %fusion.11), kind=kOutput, calls=%fused_computation.20 | convolution fusion | flops 805306368 | bytes 3145728 | tf_op jit(solution)/shard_map/dot_general | solution.py:369
  142.6 0.0 copy-done.2
  142.6 0.0 copy-start.3
  142.6 0.2 slice_select_fusion
  142.8 0.0 slice-start.2
  142.8 0.0 slice-start
  142.8 3.2 %fusion = f32[256,2048]{1,0:T(8,128)} fusion(f32[256,2048]{1,0:T(8,128)S(1)} %copy-done, f32[256,512]{1,0:T(8,128)S(1)} %slice.23, f32[2048,512]{1,0:T(8,128)S(1)} %bitcast.15, pred[2048]{0:T(1024)(128)(4,1)S(1)} %get-tuple-element.10), kind=kOutput, calls=%fused_computation.3 | convolution fusion | flops 1611661312 | bytes 8914944 | tf_op jit(solution)/shard_map/dot_general | solution.py:369
  146.1 0.0 copy-done.3
  146.1 0.0 slice-done.2
  146.1 0.0 slice-start.1
  146.1 5.6 %subtract_select_fusion = f32[512,2048]{1,0:T(8,128)} fusion(f32[512,2048]{1,0:T(8,128)S(1)} %copy-done.3, f32[512,512]{1,0:T(8,128)S(1)} %slice-done.2, f32[2048,512]{1,0:T(8,128)S(1)} %bitcast.16, pred[2048]{0:T(1024)(128)(4,1)S(1)} %get-tuple-element.10), kind=kOutput, calls=%fused_computation.1 | convolution fusion | flops 3223322624 | bytes 13633536 | tf_op jit(solution)/shard_map/dot_general | solution.py:369
  151.6 0.0 slice-done
  151.6 0.0 slice-done.1
  151.6 9.6 %select_select_fusion = f32[1024,2048]{1,0:T(8,128)} fusion(f32[1024,2048]{1,0:T(8,128)S(1)} %bitcast.19, f32[1024,512]{1,0:T(8,128)S(1)} %slice_select_fusion, pred[2048]{0:T(1024)(128)(4,1)S(1)} %get-tuple-element.10, pred[2048]{0:T(1024)(128)(4,1)S(1)} %get-tuple-element.11, pred[1024]{0:T(1024)(128)(4,1)S(1)} %broadcast_compare_fusion, ...), kind=kOutput, calls=%fused_computation | convolution fusion | flops 6450839552 | bytes 23073792 | tf_op jit(solution)/shard_map/dot_general | solution.py:369
  (6 shorter events, 0.1 us)
Async XLA Ops:
  0.7 1.6 copy-start
  132.6 3.1 %copy-start.1 = (f32[2,1280,512]{2,1,0:T(8,128)S(1)}, f32[2,1280,512]{2,1,0:T(8,128)}, u32[]{:S(2)}) copy-start(f32[2,1280,512]{2,1,0:T(8,128)} %get-tuple-element.9) | copy-start | bytes 15728644
  135.7 6.9 %copy-start.2 = (f32[1792,512]{1,0:T(8,128)}, f32[1792,512]{1,0:T(8,128)S(1)}, u32[]{:S(2)}) copy-start(f32[1792,512]{1,0:T(8,128)S(1)} %fusion.11) | copy-start | bytes 11010052
  142.6 3.5 %copy-start.3 = (f32[512,2048]{1,0:T(8,128)S(1)}, f32[512,2048]{1,0:T(8,128)}, u32[]{:S(2)}) copy-start(f32[512,2048]{1,0:T(8,128)} %train.1) | copy-start | bytes 12582916
  142.8 3.3 %slice-start.2 = ((f32[1792,512]{1,0:T(8,128)}), f32[512,512]{1,0:T(8,128)S(1)}, s32[]{:S(2)}) async-start(f32[1792,512]{1,0:T(8,128)} %copy-done.2), calls=%async_computation.2 | async-start | bytes 2097152 | tf_op jit(solution)/shard_map/slice | solution.py:383
  142.8 8.8 %slice-start = ((s8[8388608]{0:T(1024)(128)(4,1)}), s8[4194304]{0:T(1024)(128)(4,1)S(1)}, s32[]{:S(2)}) async-start(s8[8388608]{0:T(1024)(128)(4,1)} %bitcast.18), calls=%async_computation | async-start | bytes 8388608
  146.1 5.6 %slice-start.1 = ((s8[8388608]{0:T(1024)(128)(4,1)}), s8[4194304]{0:T(1024)(128)(4,1)S(1)}, s32[]{:S(2)}) async-start(s8[8388608]{0:T(1024)(128)(4,1)} %bitcast.18), calls=%async_computation.1 | async-start | bytes 8388608
